TPU v7x, 256 devices: a whole 4x4x8 slice. The times are simulated.
256 devices in a mesh: tm: 32 (over x, y, core), heads: 8 (over z).
Axes of the slice: x: 4, y: 4, z: 8, core: 2. Of those that a mesh axis runs over, the one named last changes fastest.
Arguments:
- query_raw: bfloat16 [4096, 6144], P('tm', 'heads'), may hold values from -80 to 80
- key_raw: bfloat16 [4096, 6144], P('tm', 'heads'), may hold values from -80 to 80
- values: bfloat16 [4096, 6144], P('tm', 'heads'), may hold values from -6 to 6
- forward_out: bfloat16 [4096, 6144], P('tm', 'heads'), may hold values from -1.5 to 1.5
- out_grad: bfloat16 [4096, 6144], P('tm', 'heads'), may hold values from -6 to 6
- log_sums: float32 [48, 4096], P('heads', 'tm')
- group_index: int32 [4096], replicated, may hold values from 0 to 63, never falling along the last dimension, each value on 1 to 128 neighbouring positions
- query_gain: float32 [6144], P('heads'), may hold values from 0.5 to 1.5
- key_gain: float32 [6144], P('heads'), may hold values from 0.5 to 1.5
Outputs:
- query_grad: bfloat16 [4096, 6144], P('tm', 'heads')
- key_grad: bfloat16 [4096, 6144], P('tm', 'heads')
- values_grad: bfloat16 [4096, 6144], P('tm', 'heads')
Inputs may be any that keep to these rules, and one draw needn't show every extreme that they name: `group_index`: group numbers never fall along the sequence; each group holds 1 to 128 tokens and one holds exactly 128.
All inputs are finite; a program needn't handle non-finite values.
Results may differ from a plain program's by a relative error of at most 0.012.
The roundings to bfloat16 on the way count: a program that leaves them out, or rounds other values in their place, can miss the bound.
Values may be sent and summed in bfloat16 or wider, within the bound.
A program may use at most 128 MiB of HBM per device.

v0:
```python
import math

import jax
import jax.numpy as jnp
from jax import lax
from jax.sharding import PartitionSpec as P

D = 6144
HEAD_DIM = 128


EPS = 1e-06


def in_blocks(step_fn, carried, arrays):
    piece_rows = arrays[0].shape[0]
    stacked = tuple((item.reshape((piece_rows // 512, 512) + item.shape[1:]) for item in arrays))
    offsets = jnp.arange(piece_rows // 512, dtype=jnp.int32) * 512

    def advance(state, packed):
        offset, parts = packed
        return (step_fn(state, parts, offset), None)

    carried, unused = lax.scan(advance, carried, (offsets, stacked))
    return carried


def on_device(
    query_raw, key_raw, values, forward_out, out_grad, log_sums, group_index, query_gain, key_gain
):
    tok_rows, feat_width = query_raw.shape
    heads_here = feat_width // HEAD_DIM
    score_scale = 1.0 / math.sqrt(HEAD_DIM)
    own_first = lax.axis_index("tm") * tok_rows
    own_groups = lax.dynamic_slice_in_dim(group_index, own_first, tok_rows)
    query_float = query_raw.astype(jnp.float32)
    key_float = key_raw.astype(jnp.float32)
    query_total, key_total = lax.psum(
        (jnp.sum(query_float * query_float, axis=1), jnp.sum(key_float * key_float, axis=1)),
        "heads",
    )
    query_scale = lax.rsqrt(query_total / D + EPS)
    key_scale = lax.rsqrt(key_total / D + EPS)
    query_norm = (query_float * query_scale[:, None] * query_gain).astype(jnp.bfloat16)
    key_norm = (key_float * key_scale[:, None] * key_gain).astype(jnp.bfloat16)
    query_heads = query_norm.reshape(tok_rows, heads_here, HEAD_DIM)
    key_heads = key_norm.reshape(tok_rows, heads_here, HEAD_DIM)
    value_heads = values.reshape(tok_rows, heads_here, HEAD_DIM)
    grad_heads = out_grad.reshape(tok_rows, heads_here, HEAD_DIM)
    out_dots = jnp.sum(
        (out_grad.astype(jnp.float32) * forward_out.astype(jnp.float32)).reshape(
            tok_rows, heads_here, HEAD_DIM
        ),
        axis=2,
    ).T
    all_sums, all_dots = (
        lax.all_gather(log_sums, "tm", axis=1, tiled=True),
        lax.all_gather(out_dots, "tm", axis=1, tiled=True),
    )

    def query_step(query_grads, arrays, first_row):
        key_piece, value_piece = arrays
        piece_rows = key_piece.shape[0]
        key_groups = lax.dynamic_slice_in_dim(group_index, first_row, piece_rows)

        def query_accumulate(state):
            fetched_keys = key_piece.reshape(piece_rows, heads_here, HEAD_DIM)
            fetched_values = value_piece.reshape(piece_rows, heads_here, HEAD_DIM)
            scores = (
                jnp.einsum(
                    "qhd,khd->hqk", query_heads, fetched_keys, preferred_element_type=jnp.float32
                )
                * score_scale
            )
            allowed = key_groups[None, :] <= own_groups[:, None]
            probs = jnp.exp(jnp.where(allowed[None], scores - log_sums[:, :, None], -jnp.inf))
            dprobs = jnp.einsum(
                "qhd,khd->hqk", grad_heads, fetched_values, preferred_element_type=jnp.float32
            )
            dscores = (probs * (dprobs - out_dots[:, :, None])).astype(jnp.bfloat16)
            return (
                state
                + jnp.einsum(
                    "hqk,khd->qhd", dscores, fetched_keys, preferred_element_type=jnp.float32
                )
                * score_scale
            )

        def query_unchanged(state):
            return state

        return lax.cond(
            jnp.min(key_groups) <= jnp.max(own_groups),
            query_accumulate,
            query_unchanged,
            query_grads,
        )

    def key_step(carried, arrays, first_row):
        query_piece, grad_piece = arrays
        piece_rows = query_piece.shape[0]
        query_groups = lax.dynamic_slice_in_dim(group_index, first_row, piece_rows)
        piece_sums = lax.dynamic_slice_in_dim(all_sums, first_row, piece_rows, 1)
        piece_dots = lax.dynamic_slice_in_dim(all_dots, first_row, piece_rows, 1)

        def key_accumulate(state):
            key_grads, value_grads = state
            fetched_queries = query_piece.reshape(piece_rows, heads_here, HEAD_DIM)
            fetched_grads = grad_piece.reshape(piece_rows, heads_here, HEAD_DIM)
            scores = (
                jnp.einsum(
                    "qhd,khd->hqk", fetched_queries, key_heads, preferred_element_type=jnp.float32
                )
                * score_scale
            )
            allowed = own_groups[None, :] <= query_groups[:, None]
            probs = jnp.exp(jnp.where(allowed[None], scores - piece_sums[:, :, None], -jnp.inf))
            value_grads = value_grads + jnp.einsum(
                "hqk,qhd->khd",
                probs.astype(jnp.bfloat16),
                fetched_grads,
                preferred_element_type=jnp.float32,
            )
            dprobs = jnp.einsum(
                "qhd,khd->hqk", fetched_grads, value_heads, preferred_element_type=jnp.float32
            )
            dscores = (probs * (dprobs - piece_dots[:, :, None])).astype(jnp.bfloat16)
            key_grads = (
                key_grads
                + jnp.einsum(
                    "hqk,qhd->khd", dscores, fetched_queries, preferred_element_type=jnp.float32
                )
                * score_scale
            )
            return (key_grads, value_grads)

        def key_unchanged(state):
            return state

        return lax.cond(
            jnp.min(own_groups) <= jnp.max(query_groups), key_accumulate, key_unchanged, carried
        )

    empty_grad = jnp.zeros((tok_rows, heads_here, HEAD_DIM), jnp.float32)
    query_grads = in_blocks(
        query_step,
        empty_grad,
        (
            lax.all_gather(key_norm, "tm", axis=0, tiled=True),
            lax.all_gather(values, "tm", axis=0, tiled=True),
        ),
    )
    key_grads, value_grads = in_blocks(
        key_step,
        (empty_grad, empty_grad),
        (
            lax.all_gather(query_norm, "tm", axis=0, tiled=True),
            lax.all_gather(out_grad, "tm", axis=0, tiled=True),
        ),
    )
    query_dnorm = query_grads.reshape(tok_rows, feat_width) * query_gain
    key_dnorm = key_grads.reshape(tok_rows, feat_width) * key_gain
    query_part = jnp.sum(query_float * query_dnorm, axis=1)
    key_part = jnp.sum(key_float * key_dnorm, axis=1)
    query_dot = lax.psum(query_part, "heads")
    key_dot = lax.psum(key_part, "heads")
    query_grad = (
        query_scale[:, None] * query_dnorm
        - query_float * (query_scale * query_scale * query_scale * query_dot / D)[:, None]
    )
    key_grad = (
        key_scale[:, None] * key_dnorm
        - key_float * (key_scale * key_scale * key_scale * key_dot / D)[:, None]
    )
    values_grad = value_grads.reshape(tok_rows, feat_width)
    return (
        query_grad.astype(jnp.bfloat16),
        key_grad.astype(jnp.bfloat16),
        values_grad.astype(jnp.bfloat16),
    )


def solution(mesh):
    return jax.shard_map(
        on_device,
        mesh=mesh,
        in_specs=(
            P("tm", "heads"),
            P("tm", "heads"),
            P("tm", "heads"),
            P("tm", "heads"),
            P("tm", "heads"),
            P("heads", "tm"),
            P(),
            P("heads"),
            P("heads"),
        ),
        out_specs=(P("tm", "heads"), P("tm", "heads"), P("tm", "heads")),
        check_vma=False,
    )
```

profile of v0, /device:TPU:30, one launch (start us, length us, event | category | flops | bytes accessed | tf_op | source)
XLA Modules:
  0.0 397.8 jit_solution(5856407127188190541)
XLA Ops:
  9.8 20.1 %all-reduce.1 = (f32[128]{0:T(128)S(1)}, f32[128]{0:T(128)S(1)}) all-reduce(f32[128]{0:T(128)S(1)} %fusion.26, f32[128]{0:T(128)S(1)} %fusion.20), channel_id=1, replica_groups=mesh['tm'=32,'heads'=8] {'heads'}, use_global_device_ids=true, to_apply=%region_3.0 | all-reduce | flops 256 | bytes 2048 | tf_op jit(solution)/shard_map/psum | solution.py:38
  34.2 1.8 copy.64
  38.8 24.4 %all_gather.23 = f32[6,4096]{1,0:T(8,128)} all-gather(f32[6,128]{1,0:T(8,128)S(1)} %bitcast.107), channel_id=1, replica_groups=mesh['tm'=32,'heads'=8] {'tm'}, dimensions={1}, use_global_device_ids=true | all-gather | bytes 101376 | tf_op jit(solution)/shard_map/all_gather | solution.py:58
  63.2 25.5 %all_gather.21 = f32[6,4096]{1,0:T(8,128)} all-gather(f32[6,128]{1,0:T(8,128)S(1)} %copy-done.17), channel_id=1, replica_groups=mesh['tm'=32,'heads'=8] {'tm'}, dimensions={1}, use_global_device_ids=true | all-gather | bytes 101376 | tf_op jit(solution)/shard_map/all_gather | solution.py:57
  89.3 2.0 fusion.36
  91.3 6.0 %copy.86 = bf16[96,8,8,512]{3,2,0,1:T(8,128)(2,1)} copy(bf16[96,8,8,512]{3,2,1,0:T(8,128)(2,1)} %bitcast.99) | data formatting | bytes 12582912 | tf_op jit(solution)/shard_map/reshape | solution.py:17
  97.2 46.0 %all-gather.11.cloned.1.call-done = bf16[4096,768]{1,0:T(8,128)(2,1)} async-done(((bf16[128,768]{1,0:T(8,128)(2,1)}), bf16[4096,768]{1,0:T(8,128)(2,1)}) %all-gather.11.cloned.1.call-update) | async-done | bytes 6291472 | tf_op jit(solution)/shard_map/all_gather | solution.py:158
  143.2 8.7 %copy.65 = bf16[8,512,768]{1,2,0:T(8,128)(2,1)} copy(bf16[8,512,768]{2,1,0:T(8,128)(2,1)} %bitcast.100) | data formatting | bytes 12582912 | tf_op jit(solution)/shard_map/while | solution.py:24
  152.8 56.0 %while.28 = (s32[]{:T(128)}, f32[128,6,128]{2,0,1:T(8,128)}, f32[128,6,128]{2,0,1:T(8,128)S(1)}, s32[8]{0:T(128)}, s32[4096]{0:T(1024)}, /*index=5*/s32[]{:T(128...) while((s32[]{:T(128)}, f32[128,6,128]{2,0,1:T(8,128)}, ...), condition=%wide.region_18.19_spmd, body=%wide.region_14.18_spmd.sunk | while | flops 405766656 | bytes 13974405 | solution.py:24
  201.2 7.5 %conditional.5 = ((f32[128,6,128]{2,0,1:T(8,128)}, f32[128,6,128]{2,0,1:T(8,128)S(1)})) conditional(s32[]{:T(128)} %convert_element_type.124, (f32[128,6,128]{2,0,1:T(8,128)}, f32[128,6,128]{2,0,1:T(8,128)S(1)}) %tuple.88, (s32[128]{0:T(128)}, s32[512]{0:T(512)S(1)}, bf16[8,512,768]{1,2,0:T(8,128)(2,1)}, s32[]{:T(128)}, ...), branch_computations={%region_16.16_spmd, %region_17.17_spmd} | conditional | flops 405766144 | bytes 13969980 | solution.py:140
  205.3 3.0 fusion.17
  210.0 6.1 %copy.87 = bf16[96,8,8,512]{3,2,0,1:T(8,128)(2,1)} copy(bf16[96,8,8,512]{3,2,1,0:T(8,128)(2,1)} %bitcast.97) | data formatting | bytes 12582912 | tf_op jit(solution)/shard_map/reshape | solution.py:17
  216.8 44.1 %all-gather.7.cloned.1.call-done = bf16[4096,768]{1,0:T(8,128)(2,1)} async-done(((bf16[128,768]{1,0:T(8,128)(2,1)}), bf16[4096,768]{1,0:T(8,128)(2,1)}) %all-gather.7.cloned.1.call-update) | async-done | bytes 6291472 | tf_op jit(solution)/shard_map/all_gather | solution.py:150
  261.0 8.6 %copy.59 = bf16[8,512,768]{1,2,0:T(8,128)(2,1)} copy(bf16[8,512,768]{2,1,0:T(8,128)(2,1)} %bitcast.98) | data formatting | bytes 12582912 | tf_op jit(solution)/shard_map/while | solution.py:24
  270.4 96.3 %while.27 = (s32[]{:T(128)}, f32[128,6,128]{2,0,1:T(8,128)}, s32[8]{0:T(128)}, s32[4096]{0:T(1024)}, s32[]{:T(128)}, /*index=5*/s32[128]{0:T(128)}, bf16[8,512,7...) while((s32[]{:T(128)}, f32[128,6,128]{2,0,1:T(8,128)}, ...), condition=%wide.region_10.11_spmd, body=%wide.region_6.10_spmd.sunk | while | flops 304611840 | bytes 10761033 | solution.py:24
  276.3 6.2 %conditional.4 = (f32[128,6,128]{2,0,1:T(8,128)}) conditional(s32[]{:T(128)} %convert_element_type.123, f32[128,6,128]{2,0,1:T(8,128)} %get-tuple-element.745, (s32[512]{0:T(512)S(1)}, s32[128]{0:T(128)}, bf16[8,512,768]{1,2,0:T(8,128)(2,1)}, s32[]{:T(128)}, bf16[128,6,128]{2,0,1:T(8,128)(2,1)}, /*index=5*/f32[6,128]{1,0:T(8,128)}, ...), branch_computations={%region_8.8_spmd, %region_9.9_spmd} | conditional | flops 304611328 | bytes 10756648 | solution.py:92
  279.7 2.8 fusion.5
  288.3 6.2 %conditional.4 = (f32[128,6,128]{2,0,1:T(8,128)}) conditional(s32[]{:T(128)} %convert_element_type.123, f32[128,6,128]{2,0,1:T(8,128)} %get-tuple-element.745, (s32[512]{0:T(512)S(1)}, s32[128]{0:T(128)}, bf16[8,512,768]{1,2,0:T(8,128)(2,1)}, s32[]{:T(128)}, bf16[128,6,128]{2,0,1:T(8,128)(2,1)}, /*index=5*/f32[6,128]{1,0:T(8,128)}, ...), branch_computations={%region_8.8_spmd, %region_9.9_spmd} | conditional | flops 304611328 | bytes 10756648 | solution.py:92
  291.7 2.8 fusion.5
  300.4 6.2 %conditional.4 = (f32[128,6,128]{2,0,1:T(8,128)}) conditional(s32[]{:T(128)} %convert_element_type.123, f32[128,6,128]{2,0,1:T(8,128)} %get-tuple-element.745, (s32[512]{0:T(512)S(1)}, s32[128]{0:T(128)}, bf16[8,512,768]{1,2,0:T(8,128)(2,1)}, s32[]{:T(128)}, bf16[128,6,128]{2,0,1:T(8,128)(2,1)}, /*index=5*/f32[6,128]{1,0:T(8,128)}, ...), branch_computations={%region_8.8_spmd, %region_9.9_spmd} | conditional | flops 304611328 | bytes 10756648 | solution.py:92
  303.8 2.8 fusion.5
  312.4 6.2 %conditional.4 = (f32[128,6,128]{2,0,1:T(8,128)}) conditional(s32[]{:T(128)} %convert_element_type.123, f32[128,6,128]{2,0,1:T(8,128)} %get-tuple-element.745, (s32[512]{0:T(512)S(1)}, s32[128]{0:T(128)}, bf16[8,512,768]{1,2,0:T(8,128)(2,1)}, s32[]{:T(128)}, bf16[128,6,128]{2,0,1:T(8,128)(2,1)}, /*index=5*/f32[6,128]{1,0:T(8,128)}, ...), branch_computations={%region_8.8_spmd, %region_9.9_spmd} | conditional | flops 304611328 | bytes 10756648 | solution.py:92
  315.8 2.8 fusion.5
  324.5 6.2 %conditional.4 = (f32[128,6,128]{2,0,1:T(8,128)}) conditional(s32[]{:T(128)} %convert_element_type.123, f32[128,6,128]{2,0,1:T(8,128)} %get-tuple-element.745, (s32[512]{0:T(512)S(1)}, s32[128]{0:T(128)}, bf16[8,512,768]{1,2,0:T(8,128)(2,1)}, s32[]{:T(128)}, bf16[128,6,128]{2,0,1:T(8,128)(2,1)}, /*index=5*/f32[6,128]{1,0:T(8,128)}, ...), branch_computations={%region_8.8_spmd, %region_9.9_spmd} | conditional | flops 304611328 | bytes 10756648 | solution.py:92
  327.8 2.8 fusion.5
  336.5 6.2 %conditional.4 = (f32[128,6,128]{2,0,1:T(8,128)}) conditional(s32[]{:T(128)} %convert_element_type.123, f32[128,6,128]{2,0,1:T(8,128)} %get-tuple-element.745, (s32[512]{0:T(512)S(1)}, s32[128]{0:T(128)}, bf16[8,512,768]{1,2,0:T(8,128)(2,1)}, s32[]{:T(128)}, bf16[128,6,128]{2,0,1:T(8,128)(2,1)}, /*index=5*/f32[6,128]{1,0:T(8,128)}, ...), branch_computations={%region_8.8_spmd, %region_9.9_spmd} | conditional | flops 304611328 | bytes 10756648 | solution.py:92
  339.9 2.8 fusion.5
  348.5 6.2 %conditional.4 = (f32[128,6,128]{2,0,1:T(8,128)}) conditional(s32[]{:T(128)} %convert_element_type.123, f32[128,6,128]{2,0,1:T(8,128)} %get-tuple-element.745, (s32[512]{0:T(512)S(1)}, s32[128]{0:T(128)}, bf16[8,512,768]{1,2,0:T(8,128)(2,1)}, s32[]{:T(128)}, bf16[128,6,128]{2,0,1:T(8,128)(2,1)}, /*index=5*/f32[6,128]{1,0:T(8,128)}, ...), branch_computations={%region_8.8_spmd, %region_9.9_spmd} | conditional | flops 304611328 | bytes 10756648 | solution.py:92
  351.9 2.8 fusion.5
  360.6 6.2 %conditional.4 = (f32[128,6,128]{2,0,1:T(8,128)}) conditional(s32[]{:T(128)} %convert_element_type.123, f32[128,6,128]{2,0,1:T(8,128)} %get-tuple-element.745, (s32[512]{0:T(512)S(1)}, s32[128]{0:T(128)}, bf16[8,512,768]{1,2,0:T(8,128)(2,1)}, s32[]{:T(128)}, bf16[128,6,128]{2,0,1:T(8,128)(2,1)}, /*index=5*/f32[6,128]{1,0:T(8,128)}, ...), branch_computations={%region_8.8_spmd, %region_9.9_spmd} | conditional | flops 304611328 | bytes 10756648 | solution.py:92
  363.9 2.8 fusion.5
  369.1 17.6 %all-reduce = (f32[128]{0:T(128)S(1)}, f32[128]{0:T(128)S(1)}) all-reduce(f32[128]{0:T(128)S(1)} %fusion.23, f32[128]{0:T(128)} %fusion.29), channel_id=1, replica_groups=mesh['tm'=32,'heads'=8] {'heads'}, use_global_device_ids=true, to_apply=%region_12.13 | all-reduce | flops 256 | bytes 2048 | tf_op jit(solution)/shard_map/psum | solution.py:165
  (169 shorter events, 94.9 us)
Async XLA Ops:
  7.2 26.7 %copy-start.8 = (bf16[128,768]{1,0:T(8,128)(2,1)S(1)}, bf16[128,768]{1,0:T(8,128)(2,1)}, u32[]{:S(2)}) copy-start(bf16[128,768]{1,0:T(8,128)(2,1)} %param.21) | copy-start | bytes 589828
  7.2 25.2 %copy-start.12 = (f32[768]{0:T(1024)S(1)}, f32[768]{0:T(1024)}, u32[]{:S(2)}) copy-start(f32[768]{0:T(1024)} %param.25) | copy-start | bytes 9220
  7.2 26.8 %copy-start.9 = (bf16[128,768]{1,0:T(8,128)(2,1)S(1)}, bf16[128,768]{1,0:T(8,128)(2,1)}, u32[]{:S(2)}) copy-start(bf16[128,768]{1,0:T(8,128)(2,1)} %param.19) | copy-start | bytes 589828
  7.2 84.1 %all-gather.9.cloned.1.call-start = ((), (), s32[]{:S(2)}) async-start(), calls=%async_computation.2 | async-start | bytes 6488064 | tf_op jit(solution)/shard_map/all_gather | solution.py:157
  8.5 25.8 %copy-start.1 = (bf16[128,768]{0,1:T(8,128)(2,1)}, bf16[128,768]{0,1:T(8,128)(2,1)S(1)}, u32[]{:S(2)}) copy-start(bf16[128,768]{0,1:T(8,128)(2,1)S(1)} %copy.52) | copy-start | bytes 589828
  9.7 26.5 %copy-start.3 = (bf16[128,768]{0,1:T(8,128)(2,1)}, bf16[128,768]{0,1:T(8,128)(2,1)S(1)}, u32[]{:S(2)}) copy-start(bf16[128,768]{0,1:T(8,128)(2,1)S(1)} %copy.53) | copy-start | bytes 589828
  9.7 26.3 %copy-start.10 = (bf16[128,768]{1,0:T(8,128)(2,1)S(1)}, bf16[128,768]{1,0:T(8,128)(2,1)}, u32[]{:S(2)}) copy-start(bf16[128,768]{1,0:T(8,128)(2,1)} %param.20) | copy-start | bytes 589828
  29.9 3.9 copy-start.21
  29.9 3.9 copy-start.22
  30.0 3.9 copy-start.18
  31.5 5.5 %copy-start.7 = (bf16[128,768]{0,1:T(8,128)(2,1)S(1)}, bf16[128,768]{0,1:T(8,128)(2,1)}, u32[]{:S(2)}) copy-start(bf16[128,768]{0,1:T(8,128)(2,1)} %fusion.22) | copy-start | bytes 589828
  31.5 111.7 %all-gather.11.cloned.1.call-start = ((), (), s32[]{:S(2)}) async-start(), calls=%async_computation.3 | async-start | bytes 6488064 | tf_op jit(solution)/shard_map/all_gather | solution.py:158
  32.3 177.7 %all-gather.5.cloned.1.call-start = ((), (), s32[]{:S(2)}) async-start(), calls=%async_computation | async-start | bytes 6488064 | tf_op jit(solution)/shard_map/all_gather | solution.py:149
  33.2 227.8 %all-gather.7.cloned.1.call-start = ((), (), s32[]{:S(2)}) async-start(), calls=%async_computation.1 | async-start | bytes 6488064 | tf_op jit(solution)/shard_map/all_gather | solution.py:150
  34.2 29.0 %copy-start.17 = (f32[6,128]{1,0:T(8,128)S(1)}, f32[6,128]{1,0:T(8,128)}, u32[]{:S(2)}) copy-start(f32[6,128]{1,0:T(8,128)} %param.22) | copy-start | bytes 9220
  38.7 58.5 %copy-start.15 = (f32[128,6]{0,1:T(8,128)}, f32[128,6]{0,1:T(8,128)S(1)}, u32[]{:S(2)}) copy-start(f32[128,6]{0,1:T(8,128)S(1)} %reduce_sum.47) | copy-start | bytes 9220
  201.3 3.1 copy-start.11
  209.9 6.2 %copy-start.5 = (f32[128,6,128]{0,2,1:T(8,128)}, f32[128,6,128]{0,2,1:T(8,128)S(1)}, u32[]{:S(2)}) copy-start(f32[128,6,128]{0,2,1:T(8,128)S(1)} %copy.67) | copy-start | bytes 1179652
  210.0 6.2 %copy-start.4 = (bf16[128,768]{0,1:T(8,128)(2,1)S(1)}, bf16[128,768]{0,1:T(8,128)(2,1)}, u32[]{:S(2)}) copy-start(bf16[128,768]{0,1:T(8,128)(2,1)} %copy-done.3) | copy-start | bytes 589828
  210.0 6.2 %copy-start.13 = (f32[768]{0:T(1024)S(1)}, f32[768]{0:T(1024)}, u32[]{:S(2)}) copy-start(f32[768]{0:T(1024)} %param.25) | copy-start | bytes 9220
  261.0 9.4 %copy-start.16 = (f32[128,6]{0,1:T(8,128)S(1)}, f32[128,6]{0,1:T(8,128)}, u32[]{:S(2)}) copy-start(f32[128,6]{0,1:T(8,128)} %copy-done.15) | copy-start | bytes 9220
  270.4 97.5 %copy-start.14 = (f32[768]{0:T(1024)S(1)}, f32[768]{0:T(1024)}, u32[]{:S(2)}) copy-start(f32[768]{0:T(1024)} %param.24) | copy-start | bytes 9220
  276.3 1.5 copy-start
  288.4 1.5 copy-start
  300.4 1.5 copy-start
  324.5 1.5 copy-start
  336.5 1.5 copy-start
  348.5 1.5 copy-start
  360.6 1.5 copy-start
  366.7 20.6 %copy-start.6 = (f32[128,6,128]{0,2,1:T(8,128)S(1)}, f32[128,6,128]{0,2,1:T(8,128)}, u32[]{:S(2)}) copy-start(f32[128,6,128]{0,2,1:T(8,128)} %copy-done.5) | copy-start | bytes 1179652
  366.7 22.5 %copy-start.2 = (bf16[128,768]{0,1:T(8,128)(2,1)S(1)}, bf16[128,768]{0,1:T(8,128)(2,1)}, u32[]{:S(2)}) copy-start(bf16[128,768]{0,1:T(8,128)(2,1)} %copy-done.1) | copy-start | bytes 589828
  366.7 22.5 %copy-start.19 = (f32[128]{0:T(128)S(1)}, f32[128]{0:T(128)}, u32[]{:S(2)}) copy-start(f32[128]{0:T(128)} %copy-done.18) | copy-start | bytes 1540
  (2 other events, 3.0 us)
Sparse Core Ops, SparseCore 0:
  31.6 55.2 all-gather.8
  89.5 53.6 all-gather.10
  146.3 58.5 all-gather.4
  207.2 53.7 all-gather.6
where the time goes:
time: 401 us; the launch traced here: 398 us
  waiting for transfers between devices  91.4 us (23%)
  blocking collectives  87.7 us (22%)
  local copies, waits for them, and re-layouts  77.9 us (19%)
  loops' own time  52.6 us (13%)
  other arithmetic  43.9 us (11%)
  matrix products  30.2 us (8%)
  between operations  14.1 us (4%)
    another operation x2, loops' own time, in_blocks(): carried, unused = lax.scan(advance, carried, (offsets, stacked))  52.2 us
    all_gather x1, waiting for transfers between devices, on_device(): lax.all_gather(out_grad, 'tm', axis=0, tiled=True)  46 us
    all_gather x1, waiting for transfers between devices, on_device(): lax.all_gather(values, 'tm', axis=0, tiled=True)  44.1 us
    dynamic_slice x25, local copies, waits for them, and re-layouts, in_blocks(): carried, unused = lax.scan(advance, carried, (offsets, stacked))  33.8 us
    all_gather x1, blocking collectives, on_device(): lax.all_gather(log_sums, 'tm', axis=1, tiled=True)  25.5 us
    all_gather x1, blocking collectives, on_device(): lax.all_gather(out_dots, 'tm', axis=1, tiled=True)  24.4 us
    while x9, local copies, waits for them, and re-layouts, in_blocks(): carried, unused = lax.scan(advance, carried, (offsets, stacked))  24.2 us
    dot_general x8, matrix products, query_accumulate(): jnp.einsum('hqk,khd->qhd', dscores, fetched_keys, preferred_element_type=...  22.2 us
  transfers between devices with their start and end apart: 4, of which 2 were waited for; matrix products, arithmetic and copies ran while one was open for 15% of the time, Pallas kernels for 0%

commit v1 on v0

v1 whole, which is shorter than its diff:
```python
import functools
import math

import jax
import jax.numpy as jnp
from jax import lax
from jax.experimental import pallas as pl
from jax.experimental.pallas import tpu as pltpu
from jax.sharding import PartitionSpec as P

D = 6144
HEAD_DIM = 128
EPS = 1e-06
WIN = 128
HERE = 6
WINDOWS = 32
CHUNK = 512
MESH = pl.DeviceIdType.MESH
F32 = jnp.float32
BF16 = jnp.bfloat16
LOG2E = math.log2(math.e)
SCORE_SCALE = 1.0 / math.sqrt(HEAD_DIM)
NT = (((1,), (1,)), ((), ()))
NN = (((1,), (0,)), ((), ()))


def dot(a, b, dims):
    return lax.dot_general(a, b, dims, preferred_element_type=F32)


def worker_chip(wid):
    x = wid // 3
    y = (x + 1 + wid % 3) % 4
    return 4 * x + y


def lanes_to_row(block):
    return jnp.sum(block.T, axis=0, keepdims=True)


def row_to_lanes(row):
    return jnp.broadcast_to(row, (WIN, WIN)).T


def kernel(
    q_hbm, k_hbm, v_hbm, fo_hbm, do_hbm, ls_ref, grp_ref, qg_ref, kg_ref,
    qgrad_ref, kgrad_ref, vgrad_ref,
    qraw, kraw, vraw, foraw, doraw, qn, kn, scq, sck,
    kv, qd, stats, st_src, zs, zx, acc, accq, kt, dqout, sib_out, sib_in, kvout,
    dqr, dkvr, qdn, kdn,
    load_sem, z_send, z_recv, sk, sv, sq, sd, ss, kv_recv, fwd_send, fwd_recv,
    qd_recv, st_recv, dq_send, dq_recv, sib_send, sib_recv, kvs, dkv_recv,
):
    t = lax.axis_index("tm")
    z = lax.axis_index("heads")
    chip = t // 2
    core = t % 2
    sibling = t + 1 - 2 * core
    cx = chip // 4
    cr = (chip % 4 - cx + 3) % 4
    is_worker = cr != 3
    wid = 3 * cx + cr
    head = wid // 2
    par = wid % 2

    loads = [
        pltpu.make_async_copy(src, dst, load_sem.at[i])
        for i, (src, dst) in enumerate(
            ((q_hbm, qraw), (k_hbm, kraw), (do_hbm, doraw), (fo_hbm, foraw), (v_hbm, vraw))
        )
    ]
    for c in loads:
        c.start()
    barrier = pltpu.get_barrier_semaphore()

    def greet_tm(i, _):
        pl.semaphore_signal(barrier, inc=1, device_id={"tm": (t + i) % WINDOWS}, device_id_type=MESH)
        return 0

    def greet_z(i, _):
        pl.semaphore_signal(barrier, inc=1, device_id={"heads": (z + i) % 8}, device_id_type=MESH)
        return 0

    lax.fori_loop(1, 8, greet_z, 0)
    lax.fori_loop(1, WINDOWS, greet_tm, 0)

    def cols(h):
        return slice(h * HEAD_DIM, (h + 1) * HEAD_DIM)

    loads[0].wait()
    loads[1].wait()
    zs[...] = jnp.zeros_like(zs)
    for row, raw in ((0, qraw), (1, kraw)):
        total = jnp.zeros((WIN, WIN), F32)
        for h in range(HERE):
            x = raw[:, cols(h)].astype(F32)
            total = total + x * x
        zs[0, row : row + 1, :] = lanes_to_row(total)

    loads[2].wait()
    loads[3].wait()
    own = grp_ref[pl.ds(t, 1), :].astype(F32)
    nxt = grp_ref[pl.ds(jnp.minimum(t + 1, WINDOWS - 1), 1), :].astype(F32)
    seen = (row_to_lanes(own) <= own).astype(F32)
    seen_next = jnp.where(
        (t < WINDOWS - 1) & (row_to_lanes(nxt) <= own), 1.0, 0.0
    )
    last = (t * WIN - 1).astype(F32) + jnp.sum(seen + seen_next, axis=0, keepdims=True)
    st_src[...] = jnp.zeros_like(st_src)
    for h in range(HERE):
        prod = doraw[:, cols(h)].astype(F32) * foraw[:, cols(h)].astype(F32)
        st_src[h, 0:1, :] = ls_ref[h : h + 1, :] * LOG2E
        st_src[h, 1:2, :] = lanes_to_row(prod)
        st_src[h, 2:3, :] = last
    loads[4].wait()

    pl.semaphore_wait(barrier, WINDOWS - 1 + 7)

    def exchange_z(which):
        def send(i, _):
            pltpu.make_async_remote_copy(
                src_ref=zs.at[which], dst_ref=zx.at[which, z],
                send_sem=z_send.at[which, i], recv_sem=z_recv.at[which],
                device_id={"heads": (z + i) % 8}, device_id_type=MESH,
            ).start()
            return 0

        lax.fori_loop(1, 8, send, 0)
        zx[which, pl.ds(z, 1)] = zs[pl.ds(which, 1)]

    def exchange_z_wait(which):
        part = zx.at[which, pl.ds(0, 7)]
        pltpu.make_async_copy(part, part, z_recv.at[which]).wait()
        return jnp.sum(zx[which], axis=0)

    exchange_z(0)

    def put(src, dst, send_sem, recv_sem, target):
        @pl.when(target == t)
        def _():
            pltpu.make_async_copy(src, dst, recv_sem).start()

        @pl.when(target != t)
        def _():
            pltpu.make_async_remote_copy(
                src_ref=src, dst_ref=dst, send_sem=send_sem, recv_sem=recv_sem,
                device_id={"tm": target}, device_id_type=MESH,
            ).start()

    def put_wait(src, send_sem, target):
        @pl.when(target != t)
        def _():
            pltpu.make_async_copy(src, src, send_sem).wait()

    own_par = t % 2
    own_slot = t // 2
    own_pair = t // 4
    own_core = (t // 2 + t // 4) % 2
    first = (t * HERE) // WINDOWS

    def head_cols(h):
        return pl.ds(pl.multiple_of(h * HEAD_DIM, HEAD_DIM), HEAD_DIM)

    def key_target(h, which):
        return 2 * worker_chip(2 * h + own_par) + which

    def query_target(h, which):
        return 2 * worker_chip(2 * h + which) + own_core

    def send_keys(src, which, sems):
        def step(i, _):
            h = (first + i) % HERE
            put(
                src.at[:, head_cols(h)],
                kv.at[which, pl.ds(pl.multiple_of(own_slot * WIN, WIN), WIN), :],
                sems.at[h], kv_recv, key_target(h, which),
            )
            return 0

        lax.fori_loop(0, HERE, step, 0)

    def send_queries(src, which, sems):
        def step(i, _):
            h = ((first + i // 2) % HERE)
            to = i % 2
            put(
                src.at[:, head_cols(h)],
                qd.at[own_pair, which, pl.ds(pl.multiple_of(own_par * WIN, WIN), WIN), :],
                sems.at[h, to], qd_recv.at[own_pair], query_target(h, to),
            )
            return 0

        lax.fori_loop(0, 2 * HERE, step, 0)

    def send_stats():
        def step(i, _):
            h = ((first + i // 2) % HERE)
            to = i % 2
            put(
                st_src.at[h],
                stats.at[own_pair, :, pl.ds(pl.multiple_of(own_par * WIN, WIN), WIN)],
                ss.at[h, to], st_recv.at[own_pair], query_target(h, to),
            )
            return 0

        lax.fori_loop(0, 2 * HERE, step, 0)

    send_keys(vraw, 1, sv)
    send_stats()
    send_queries(doraw, 1, sd)

    totals = exchange_z_wait(0)
    scales = lax.rsqrt(totals / D + EPS)
    scq[...] = row_to_lanes(scales[0:1, :])
    sck[...] = row_to_lanes(scales[1:2, :])
    for h in range(HERE):
        kn[:, cols(h)] = (kraw[:, cols(h)].astype(F32) * sck[...] * kg_ref[:, cols(h)]).astype(BF16)
    send_keys(kn, 0, sk)
    for h in range(HERE):
        qn[:, cols(h)] = (qraw[:, cols(h)].astype(F32) * scq[...] * qg_ref[:, cols(h)]).astype(BF16)
    send_queries(qn, 0, sq)

    @pl.when(is_worker)
    def _():
        acc[...] = jnp.zeros_like(acc)
        mine = kv.at[core]
        pltpu.make_async_copy(mine, mine, kv_recv).wait()
        forward = pltpu.make_async_remote_copy(
            src_ref=kv.at[core], dst_ref=kv.at[core], send_sem=fwd_send, recv_sem=fwd_recv,
            device_id={"tm": sibling}, device_id_type=MESH,
        )
        forward.start()
        forward.wait_recv()

        def turn(i, _):
            rows = pl.ds(pl.multiple_of(i * WIN, WIN), WIN)
            kt[:, rows] = kv[0, rows, :].T
            return 0

        lax.fori_loop(0, 16, turn, 0)
        start = ((head + 1) * 4) // 3 - 1

        def pair_step(i, _):
            m = (start - i + 8) % 8
            p = 2 * m + (core + m) % 2
            pltpu.make_async_copy(stats.at[m], stats.at[m], st_recv.at[m]).wait()
            pltpu.make_async_copy(qd.at[m], qd.at[m], qd_recv.at[m]).wait()
            accq[...] = jnp.zeros_like(accq)

            def chunk_step(c, _):
                rows = pl.ds(pl.multiple_of(c * CHUNK, CHUNK), CHUNK)
                q = qd[m, 0]
                do = qd[m, 1]
                s = dot(kv[0, rows, :], q, NT)
                probs = jnp.exp2(s * (SCORE_SCALE * LOG2E) - stats[m, 0:1, :])
                r = lax.broadcasted_iota(jnp.int32, (CHUNK, 2 * WIN), 0)
                place = (r + WIN * (r // WIN) + (c * 2 * CHUNK + par * WIN)).astype(F32)
                probs = jnp.where(place <= stats[m, 2:3, :], probs, 0.0)
                dp = dot(kv[1, rows, :], do, NT)
                ds = (probs * (dp - stats[m, 1:2, :])).astype(BF16)
                acc[1, rows, :] += dot(probs.astype(BF16), do, NN)
                acc[0, rows, :] += dot(ds, q, NN)
                accq[...] += dot(kt[:, rows], ds, NN)
                return 0

            steps = (jnp.minimum((p + 2) * WIN, 2048) + CHUNK - 1) // CHUNK
            lax.fori_loop(0, steps, chunk_step, 0)
            dqout[m] = accq[...].T.astype(BF16)

            def back(j, _):
                put(
                    dqout.at[m, pl.ds(pl.multiple_of(j * WIN, WIN), WIN), :],
                    dqr.at[head, par], dq_send.at[m, j], dq_recv, 2 * p + j,
                )
                return 0

            lax.fori_loop(0, 2, back, 0)
            return 0

        lax.fori_loop(0, 8, pair_step, 0)

        sib_out[...] = acc[1 - core].astype(BF16)
        swap = pltpu.make_async_remote_copy(
            src_ref=sib_out, dst_ref=sib_in, send_sem=sib_send, recv_sem=sib_recv,
            device_id={"tm": sibling}, device_id_type=MESH,
        )
        swap.start()
        swap.wait_recv()
        kvout[...] = (acc[core] + sib_in[...].astype(F32)).astype(BF16)

        def back(i, _):
            put(
                kvout.at[pl.ds(pl.multiple_of(i * WIN, WIN), WIN), :],
                dkvr.at[core, head], kvs.at[i], dkv_recv.at[core], 2 * i + par,
            )
            return 0

        lax.fori_loop(0, 16, back, 0)
        forward.wait_send()
        swap.wait_send()

        def back_wait(i, _):
            put_wait(kvout.at[pl.ds(0, WIN), :], kvs.at[i], 2 * i + par)
            return 0

        lax.fori_loop(0, 16, back_wait, 0)

        def dq_wait(i, _):
            m = i // 2
            put_wait(
                dqout.at[0, pl.ds(0, WIN), :], dq_send.at[m, i % 2],
                2 * (2 * m + (core + m) % 2) + i % 2,
            )
            return 0

        lax.fori_loop(0, 16, dq_wait, 0)

    pltpu.make_async_copy(dqr, dqr, dq_recv).wait()
    part = jnp.zeros((WIN, WIN), F32)
    for h in range(HERE):
        d = (dqr[h, 0].astype(F32) + dqr[h, 1].astype(F32)) * SCORE_SCALE * qg_ref[:, cols(h)]
        qdn[:, cols(h)] = d
        part = part + qraw[:, cols(h)].astype(F32) * d
    zs[1, 0:1, :] = lanes_to_row(part)
    pltpu.make_async_copy(dkvr.at[0], dkvr.at[0], dkv_recv.at[0]).wait()
    part = jnp.zeros((WIN, WIN), F32)
    for h in range(HERE):
        d = dkvr[0, h].astype(F32) * SCORE_SCALE * kg_ref[:, cols(h)]
        kdn[:, cols(h)] = d
        part = part + kraw[:, cols(h)].astype(F32) * d
    zs[1, 1:2, :] = lanes_to_row(part)
    exchange_z(1)
    pltpu.make_async_copy(dkvr.at[1], dkvr.at[1], dkv_recv.at[1]).wait()
    for h in range(HERE):
        vgrad_ref[:, cols(h)] = dkvr[1, h]
    dots = exchange_z_wait(1) / D
    cq = row_to_lanes(dots[0:1, :])
    ck = row_to_lanes(dots[1:2, :])
    for sc, cc, raw, dn, out in (
        (scq, cq, qraw, qdn, qgrad_ref), (sck, ck, kraw, kdn, kgrad_ref),
    ):
        s = sc[...]
        coef = s * s * s * cc
        for h in range(HERE):
            out[:, cols(h)] = (s * dn[:, cols(h)] - raw[:, cols(h)].astype(F32) * coef).astype(BF16)

    def z_wait(i, _):
        for which in range(2):
            pltpu.make_async_copy(zs.at[which], zs.at[which], z_send.at[which, i]).wait()
        return 0

    lax.fori_loop(1, 8, z_wait, 0)
    block = kn.at[:, pl.ds(0, HEAD_DIM)]

    def send_wait(h, _):
        put_wait(block, sk.at[h], key_target(h, 0))
        put_wait(block, sv.at[h], key_target(h, 1))
        for to in range(2):
            put_wait(block, sq.at[h, to], query_target(h, to))
            put_wait(block, sd.at[h, to], query_target(h, to))
            put_wait(st_src.at[0], ss.at[h, to], query_target(h, to))
        return 0

    lax.fori_loop(0, HERE, send_wait, 0)


def on_device(q, k, v, fo, do, log_sums, group_index, q_gain, k_gain):
    block = (WIN, HERE * HEAD_DIM)
    any_spec = pl.BlockSpec(memory_space=pl.ANY)
    vmem_spec = pl.BlockSpec(memory_space=pltpu.VMEM)
    dma = pltpu.SemaphoreType.DMA
    return pl.pallas_call(
        kernel,
        out_shape=[jax.ShapeDtypeStruct(block, BF16)] * 3,
        in_specs=[any_spec] * 5 + [vmem_spec] * 4,
        out_specs=[vmem_spec] * 3,
        scratch_shapes=[
            *[pltpu.VMEM(block, BF16)] * 7,
            pltpu.VMEM((WIN, WIN), F32),
            pltpu.VMEM((WIN, WIN), F32),
            pltpu.VMEM((2, 2048, HEAD_DIM), BF16),
            pltpu.VMEM((8, 2, 2 * WIN, HEAD_DIM), BF16),
            pltpu.VMEM((8, 8, 2 * WIN), F32),
            pltpu.VMEM((HERE, 8, WIN), F32),
            pltpu.VMEM((2, 8, WIN), F32),
            pltpu.VMEM((2, 8, 8, WIN), F32),
            pltpu.VMEM((2, 2048, HEAD_DIM), F32),
            pltpu.VMEM((HEAD_DIM, 2 * WIN), F32),
            pltpu.VMEM((HEAD_DIM, 2048), BF16),
            pltpu.VMEM((8, 2 * WIN, HEAD_DIM), BF16),
            pltpu.VMEM((2048, HEAD_DIM), BF16),
            pltpu.VMEM((2048, HEAD_DIM), BF16),
            pltpu.VMEM((2048, HEAD_DIM), BF16),
            pltpu.VMEM((HERE, 2, WIN, HEAD_DIM), BF16),
            pltpu.VMEM((2, HERE, WIN, HEAD_DIM), BF16),
            pltpu.VMEM(block, F32),
            pltpu.VMEM(block, F32),
            dma((5,)), dma((2, 8)), dma((2,)),
            dma((HERE,)), dma((HERE,)), dma((HERE, 2)), dma((HERE, 2)), dma((HERE, 2)),
            dma, dma, dma,
            dma((8,)), dma((8,)), dma((8, 2)), dma, dma, dma, dma((16,)), dma((2,)),
        ],
        compiler_params=pltpu.CompilerParams(
            collective_id=0, has_side_effects=True, vmem_limit_bytes=40 << 20
        ),
        cost_estimate=pl.CostEstimate(
            flops=2 * 10**9, bytes_accessed=2 * 10**6, transcendentals=2 * 10**6
        ),
    )(
        q, k, v, fo, do, log_sums, group_index.reshape(WINDOWS, WIN),
        q_gain.reshape(1, -1), k_gain.reshape(1, -1),
    )


def solution(mesh):
    tok, heads = P("tm", "heads"), P("heads")
    return jax.shard_map(
        on_device,
        mesh=mesh,
        in_specs=(tok, tok, tok, tok, tok, P("heads", "tm"), P(), heads, heads),
        out_specs=(tok, tok, tok),
        check_vma=False,
    )
```

time: 401 us -> 72.5 us (0.18)
  the two profiles are of different devices: /device:TPU:30 before, /device:TPU:4 now
where the time goes in v1:
time: 72.5 us; the launch traced here: 72.2 us
  Pallas kernels  62.8 us (87%)
  local copies, waits for them, and re-layouts  8.76 us (12%)
    pallas_call x1, Pallas kernels, on_device(): pl.pallas_call(kernel, out_shape=[jax.ShapeDtypeStruct(block, BF16)] * 3,...  62.8 us
    unnamed x19, local copies, waits for them, and re-layouts  8.07 us

profile of v1, /device:TPU:4, one launch (start us, length us, event | category | flops | bytes accessed | tf_op | source)
XLA Modules:
  0.0 72.2 jit_solution(6203579657633562223)
XLA Ops:
  0.6 0.0 copy-start.7
  0.6 0.7 reshape.16.qg_ref
  1.3 0.0 copy-done.7
  1.3 0.0 copy-start.6
  1.3 0.7 copy-done.6
  2.0 0.0 copy-start
  2.0 0.9 %copy-done = bf16[128,768]{1,0:T(8,128)(2,1)S(1)} copy-done((bf16[128,768]{1,0:T(8,128)(2,1)S(1)}, bf16[128,768]{1,0:T(8,128)(2,1)}, u32[]{:S(2)}) %copy-start) | copy-done | bytes 196632
  3.0 0.0 copy-start.1
  3.0 0.9 %copy-done.1 = bf16[128,768]{1,0:T(8,128)(2,1)S(1)} copy-done((bf16[128,768]{1,0:T(8,128)(2,1)S(1)}, bf16[128,768]{1,0:T(8,128)(2,1)}, u32[]{:S(2)}) %copy-start.1) | copy-done | bytes 196632
  3.9 0.0 copy-start.2
  3.9 0.9 %copy-done.2 = bf16[128,768]{1,0:T(8,128)(2,1)S(1)} copy-done((bf16[128,768]{1,0:T(8,128)(2,1)S(1)}, bf16[128,768]{1,0:T(8,128)(2,1)}, u32[]{:S(2)}) %copy-start.2) | copy-done | bytes 196632
  4.8 0.0 copy-start.3
  4.8 0.9 %copy-done.3 = bf16[128,768]{1,0:T(8,128)(2,1)S(1)} copy-done((bf16[128,768]{1,0:T(8,128)(2,1)S(1)}, bf16[128,768]{1,0:T(8,128)(2,1)}, u32[]{:S(2)}) %copy-start.3) | copy-done | bytes 196632
  5.7 0.0 copy-start.4
  5.7 0.9 %copy-done.4 = bf16[128,768]{1,0:T(8,128)(2,1)S(1)} copy-done((bf16[128,768]{1,0:T(8,128)(2,1)S(1)}, bf16[128,768]{1,0:T(8,128)(2,1)}, u32[]{:S(2)}) %copy-start.4) | copy-done | bytes 196632
  6.7 0.0 copy-start.5
  6.7 0.7 copy-done.5
  7.4 62.8 %shard_map.112 = (bf16[128,768]{1,0:T(8,128)(2,1)S(1)}, bf16[128,768]{1,0:T(8,128)(2,1)S(1)}, bf16[128,768]{1,0:T(8,128)(2,1)S(1)}) custom-call(bf16[128,768]{1,0:T(8,128)(2,1)S(1)} %copy-done, bf16[128,768]{1,0:T(8,128)(2,1)S(1)} %copy-done.1, bf16[128,768]{1,0:T(8,128)(2,1)S(1)} %copy-done.2, bf16[128,768]{1,0:T(8,128)(2,1)S(1)} %copy-done.3, ...), custom_call_target="tpu_custom_call" | custom-call | flops 2000000000 | bytes 2000000 | tf_op jit(solution)/shard_map/pallas_call | solution.py:372
  70.2 0.7 copy.15
  70.8 0.7 copy.16
  71.5 0.7 copy.17
  (1 shorter events, 0.0 us)
Async XLA Ops:
  0.6 0.7 copy-start.7
  1.3 0.7 copy-start.6
  2.0 0.9 %copy-start = (bf16[128,768]{1,0:T(8,128)(2,1)S(1)}, bf16[128,768]{1,0:T(8,128)(2,1)}, u32[]{:S(2)}) copy-start(bf16[128,768]{1,0:T(8,128)(2,1)} %q_hbm.1) | copy-start | bytes 589828
  3.0 0.9 %copy-start.1 = (bf16[128,768]{1,0:T(8,128)(2,1)S(1)}, bf16[128,768]{1,0:T(8,128)(2,1)}, u32[]{:S(2)}) copy-start(bf16[128,768]{1,0:T(8,128)(2,1)} %k_hbm.1) | copy-start | bytes 589828
  3.9 0.9 %copy-start.2 = (bf16[128,768]{1,0:T(8,128)(2,1)S(1)}, bf16[128,768]{1,0:T(8,128)(2,1)}, u32[]{:S(2)}) copy-start(bf16[128,768]{1,0:T(8,128)(2,1)} %v_hbm.1) | copy-start | bytes 589828
  4.8 0.9 %copy-start.3 = (bf16[128,768]{1,0:T(8,128)(2,1)S(1)}, bf16[128,768]{1,0:T(8,128)(2,1)}, u32[]{:S(2)}) copy-start(bf16[128,768]{1,0:T(8,128)(2,1)} %fo_hbm.1) | copy-start | bytes 589828
  5.7 0.9 %copy-start.4 = (bf16[128,768]{1,0:T(8,128)(2,1)S(1)}, bf16[128,768]{1,0:T(8,128)(2,1)}, u32[]{:S(2)}) copy-start(bf16[128,768]{1,0:T(8,128)(2,1)} %do_hbm.1) | copy-start | bytes 589828
  6.7 0.7 copy-start.5

commit v2 on v1

v2 whole, which is shorter than its diff:
```python
import functools
import math

import jax
import jax.numpy as jnp
from jax import lax
from jax.experimental import pallas as pl
from jax.experimental.pallas import tpu as pltpu
from jax.sharding import PartitionSpec as P

D = 6144
HEAD_DIM = 128
EPS = 1e-06
WIN = 128
HERE = 6
WINDOWS = 32
BLOCKS = WINDOWS // 2
KEYS = BLOCKS * WIN
LEAD = 4
WINDOW = 2
LAG = 2
PAIRS = 8
MESH = pl.DeviceIdType.MESH
F32 = jnp.float32
BF16 = jnp.bfloat16
LOG2E = math.log2(math.e)
SCORE_SCALE = 1.0 / math.sqrt(HEAD_DIM)
NT = (((1,), (1,)), ((), ()))
NN = (((1,), (0,)), ((), ()))


def dot(a, b, dims):
    return lax.dot_general(a, b, dims, preferred_element_type=F32)


def worker_at(x, y):
    turn = (y - x + 3) % 4
    middle = turn % 2
    head = middle * (4 + x // 2) + (1 - middle) * x
    part = middle * (1 - x % 2) + (1 - middle) * (1 - turn // 2)
    return turn != 3, head, part


def across(y, k):
    return (y // 2 + k // 2) % 2 * 2 + (y + k) % 2


def lanes_to_row(block):
    return jnp.sum(block.T, axis=0, keepdims=True)


def row_to_lanes(row):
    return jnp.broadcast_to(row, (WIN, WIN)).T


def kernel(
    q_hbm, k_hbm, v_hbm, fo_hbm, do_hbm, ls_hbm, grp_hbm, qg_hbm, kg_hbm,
    qgrad_ref, kgrad_ref, vgrad_ref,
    qraw, kraw, vraw, foraw, doraw, qn, scq, sck,
    kv, qd, stats, st_src, zs, zx, acc, accq, kt, dqout, sib_out, sib_in, kvout,
    dqr, dkvr, qdn, kdn,
    place, k_rows, kst_src, gains, spare16, spare32, ls_ref, grp_ref, qg_ref, kg_ref,
    load_sem, z_send, z_recv, sk, sv, sq, ss, sks, kst_recv, kv_recv, fwd_send, fwd_recv,
    qd_recv, st_recv, dq_send, dq_recv, sib_send, sib_recv, kvs, dkv_recv,
):
    t = lax.axis_index("tm")
    z = lax.axis_index("heads")
    chip = t // 2
    core = t % 2
    sibling = t + 1 - 2 * core
    cx = chip // 4
    cy = chip % 4
    is_worker, head, par = worker_at(cx, cy)

    loads = [
        pltpu.make_async_copy(src, dst, load_sem.at[i])
        for i, (src, dst) in enumerate(
            (
                (q_hbm, qraw), (k_hbm, kraw), (do_hbm, doraw), (fo_hbm, foraw), (v_hbm, vraw),
                (ls_hbm, ls_ref), (grp_hbm, grp_ref), (qg_hbm, qg_ref), (kg_hbm, kg_ref),
            )
        )
    ]
    for c in loads:
        c.start()
    barrier = pltpu.get_barrier_semaphore()

    def greet_tm(i, _):
        pl.semaphore_signal(barrier, inc=1, device_id={"tm": (t + i) % WINDOWS}, device_id_type=MESH)
        return 0

    def greet_z(i, _):
        pl.semaphore_signal(barrier, inc=1, device_id={"heads": (z + i) % 8}, device_id_type=MESH)
        return 0

    with jax.named_scope("greet"):
        lax.fori_loop(1, 8, greet_z, 0)
        lax.fori_loop(1, WINDOWS, greet_tm, 0)

    def cols(h):
        return slice(h * HEAD_DIM, (h + 1) * HEAD_DIM)

    def gain(ref, h):
        return ref[pl.ds(h * HEAD_DIM, HEAD_DIM)].reshape(1, HEAD_DIM)

    with jax.named_scope("sums"):
        loads[0].wait()
        loads[1].wait()
        zs[...] = jnp.zeros_like(zs)
        for row, raw in ((0, qraw), (1, kraw)):
            total = jnp.zeros((WIN, WIN), F32)
            for h in range(HERE):
                x = raw[:, cols(h)].astype(F32)
                total = total + x * x
            zs[0, row : row + 1, :] = lanes_to_row(total)

    with jax.named_scope("rowdata"):
        loads[2].wait()
        loads[3].wait()
        loads[5].wait()
        loads[6].wait()
        own = grp_ref[pl.ds(t, 1), :].astype(F32)
        nxt = grp_ref[pl.ds(jnp.minimum(t + 1, WINDOWS - 1), 1), :].astype(F32)
        seen = (row_to_lanes(own) <= own).astype(F32)
        seen_next = jnp.where(
            (t < WINDOWS - 1) & (row_to_lanes(nxt) <= own), 1.0, 0.0
        )
        last = (t * WIN - 1).astype(F32) + jnp.sum(seen + seen_next, axis=0, keepdims=True)
        st_src[...] = jnp.zeros_like(st_src)
        for h in range(HERE):
            prod = doraw[:, cols(h)].astype(F32) * foraw[:, cols(h)].astype(F32)
            st_src[h, 0:1, :] = ls_ref[h : h + 1, :] * LOG2E
            st_src[h, 1:2, :] = lanes_to_row(prod)
            st_src[h, 2:3, :] = last
        loads[4].wait()
        loads[7].wait()
        loads[8].wait()

    with jax.named_scope("meet"):
        pl.semaphore_wait(barrier, WINDOWS - 1 + 7)

    def exchange_z(which):
        def send(i, _):
            pltpu.make_async_remote_copy(
                src_ref=zs.at[which], dst_ref=zx.at[which, z],
                send_sem=z_send.at[which], recv_sem=z_recv.at[which],
                device_id={"heads": (z + i) % 8}, device_id_type=MESH,
            ).start()
            return 0

        lax.fori_loop(1, 8, send, 0)
        zx[which, pl.ds(z, 1)] = zs[pl.ds(which, 1)]

    def exchange_z_wait(which):
        part = zx.at[which, pl.ds(0, 7)]
        pltpu.make_async_copy(part, part, z_recv.at[which]).wait()
        return jnp.sum(zx[which], axis=0)

    exchange_z(0)

    def put(src, dst, send_sem, recv_sem, target, spare):
        @pl.when(target == t)
        def _():
            pltpu.make_async_copy(src, dst, recv_sem).start()
            pltpu.make_async_copy(src, spare, send_sem).start()

        @pl.when(target != t)
        def _():
            pltpu.make_async_remote_copy(
                src_ref=src, dst_ref=dst, send_sem=send_sem, recv_sem=recv_sem,
                device_id={"tm": target}, device_id_type=MESH,
            ).start()

    def wait_for(ref, sem):
        pltpu.make_async_copy(ref, ref, sem).wait()

    def rows_of(i, size=WIN):
        return pl.ds(pl.multiple_of(i * size, size), size)

    def head_cols(h):
        return pl.ds(pl.multiple_of(h * HEAD_DIM, HEAD_DIM), HEAD_DIM)

    own_part = t % 2
    own_slot = t // 2
    own_pair = t // 4
    own_core = (t // 2 + t // 4) % 2

    def for_workers(do):
        def step(i, _):
            x = (cx + i // 4) % 4
            y = (cy + i % 4) % 4
            there, h, part = worker_at(x, y)
            pl.when(there)(functools.partial(do, 2 * (4 * x + y), h, part))
            return 0

        lax.fori_loop(0, 16, step, 0)

    def send_keys(base, h, part):
        @pl.when(part == own_part)
        def _():
            for which, src, sem in ((0, kraw, sk), (1, vraw, sv)):
                put(
                    src.at[:, head_cols(h)], kv.at[which, rows_of(own_slot), :],
                    sem, kv_recv.at[own_slot // 2], base + which, spare16.at[which],
                )

    def send_rows(base, h, part):
        @pl.when(part == own_part)
        def _():
            put(kst_src, k_rows.at[own_slot], sks, kst_recv, base, spare32.at[0])

        put(
            st_src.at[h], stats.at[own_pair, :, rows_of(t % 2)],
            ss, st_recv, base + own_core, spare32.at[1],
        )

    def send_queries(base, h, part, sem):
        for which, src in ((1, doraw), (0, qn)):
            put(
                src.at[:, head_cols(h)], qd.at[own_pair, which, rows_of(t % 2), :],
                sem, qd_recv.at[own_pair], base + own_core, spare16.at[2 + which],
            )

    with jax.named_scope("send_kv"):
        for_workers(send_keys)

    with jax.named_scope("wait_z"):
        totals = exchange_z_wait(0)
    with jax.named_scope("send_q"):
        scales = lax.rsqrt(totals / D + EPS)
        kst_src[...] = scales
        for_workers(send_rows)
        scq[...] = row_to_lanes(scales[0:1, :])
        sck[...] = row_to_lanes(scales[1:2, :])
        for h in range(HERE):
            gains[h : h + 1, :] = gain(kg_ref, h)
            qn[:, cols(h)] = (qraw[:, cols(h)].astype(F32) * scq[...] * gain(qg_ref, h)).astype(BF16)


    def turn(j, do):
        for k in range(2):
            x = (cx + j // 2) % 4
            y = across(cy, 2 * (j % 2) + k)
            there, h, part = worker_at(x, y)
            pl.when(there)(functools.partial(do, 2 * (4 * x + y), h, part, sq.at[j, k]))

    def turn_sent(j, _):
        turn(j, lambda base, h, part, sem: wait_for(qd.at[0, 0], sem))
        return 0

    def send_turn(j, _):
        @pl.when(j >= WINDOW)
        def _():
            turn_sent(j - WINDOW, 0)

        turn(j, send_queries)
        return 0

    with jax.named_scope("hold"):
        wait_for(kraw, sk)
        wait_for(vraw, sv)
    with jax.named_scope("send_q0"):
        lax.fori_loop(0, jnp.where(is_worker, LEAD, PAIRS), send_turn, 0)

    @pl.when(is_worker)
    def _():
        with jax.named_scope("wait_kv"):
            acc[...] = jnp.zeros_like(acc)
            r = lax.broadcasted_iota(jnp.int32, (512, WIN), 0)
            place[...] = (r + WIN * (r // WIN)).astype(F32)

            @pl.when(core == 0)
            def _():
                wait_for(k_rows, kst_recv)

            def forward(c, _):
                piece = kv.at[core, rows_of(c, 256), :]
                wait_for(piece, kv_recv.at[c])

                @pl.when(core == 0)
                def _():
                    for j in range(2):
                        i = 2 * c + j
                        scale = row_to_lanes(k_rows[i, 1:2, :])
                        normed = kv[0, rows_of(i), :].astype(F32) * scale * gains[pl.ds(head, 1), :]
                        kv[0, rows_of(i), :] = normed.astype(BF16)

                pltpu.make_async_remote_copy(
                    src_ref=piece, dst_ref=piece, send_sem=fwd_send, recv_sem=fwd_recv.at[c],
                    device_id={"tm": sibling}, device_id_type=MESH,
                ).start()
                return 0

            lax.fori_loop(0, BLOCKS // 2, forward, 0)

        with jax.named_scope("forward"):

            def forwarded(c, _):
                rows = rows_of(c, 256)
                wait_for(kv.at[1 - core, rows, :], fwd_recv.at[c])
                kt[:, rows] = kv[0, rows, :].T
                return 0

            lax.fori_loop(0, BLOCKS // 2, forwarded, 0)
            wait_for(stats, st_recv)

        def give(c, _):
            sib_out[rows_of(c, 256), :] = acc[1 - core, rows_of(c, 256), :].astype(BF16)
            pltpu.make_async_remote_copy(
                src_ref=sib_out.at[rows_of(c, 256), :], dst_ref=sib_in.at[rows_of(c, 256), :],
                send_sem=sib_send, recv_sem=sib_recv.at[c],
                device_id={"tm": sibling}, device_id_type=MESH,
            ).start()
            return 0

        def finish(c, _):
            rows = rows_of(c, 256)
            pltpu.make_async_copy(sib_in.at[rows, :], sib_in.at[rows, :], sib_recv.at[c]).wait()
            kvout[rows, :] = (acc[core, rows, :] + sib_in[rows, :].astype(F32)).astype(BF16)
            for j in range(2):
                i = 2 * c + j
                put(
                    kvout.at[rows_of(i), :], dkvr.at[core, head],
                    kvs, dkv_recv.at[core], 2 * i + par, spare16.at[5],
                )
            return 0

        def row_of(i):
            return (cx - i // 2 + 4) % 4

        def pair_of(i):
            return 2 * row_of(i) + (cy // 2 + i) % 2

        def done_after(i):
            r = row_of(i)
            ready = ((r > cx) | (cx == 3)).astype(jnp.int32) * (i % 2)
            end = i // (PAIRS - 1)
            lo = ready * (1 - end) * (2 * r + 1 - par)
            hi = ready * jnp.minimum(2 * r + 3 - par, BLOCKS // 2)
            return lo, hi

        def finish_all(lo, hi):
            count = jnp.maximum(hi - lo, 1)
            lax.fori_loop(lo, hi, lambda c, _: finish(lo + (c - lo + 2 * cx) % count, _), 0)

        def pair_step(i, _):
            m = pair_of(i)

            @pl.when(i + LEAD < PAIRS)
            def _():
                send_turn(i + LEAD, 0)

            p = 2 * m + (core + m) % 2
            with jax.named_scope("wait_qd"):
                wait_for(qd.at[m], qd_recv.at[m])
            accq[...] = jnp.zeros_like(accq)

            def work(row, size, edge):
                rows = pl.ds(pl.multiple_of(row, 256), size)
                q = qd[m, 0]
                do = qd[m, 1]
                s = dot(kv[0, rows, :], q, NT)
                probs = jnp.exp2(s * (SCORE_SCALE * LOG2E) - stats[m, 0:1, :])
                if edge:
                    limit = stats[m, 2:3, :] - (2 * row + par * WIN).astype(F32)
                    at = place[:size, :]
                    probs = jnp.where(jnp.concatenate([at, at], axis=1) <= limit, probs, 0.0)
                dp = dot(kv[1, rows, :], do, NT)
                ds = (probs * (dp - stats[m, 1:2, :])).astype(BF16)
                acc[1, rows, :] += dot(probs.astype(BF16), do, NN)
                acc[0, rows, :] += dot(ds, q, NN)
                accq[...] += dot(kt[:, rows], ds, NN)

            chunks = jnp.minimum((p + 3 - par) // 2, BLOCKS // 2)
            inner = p // 4 * 2
            rest = chunks - inner

            def whole(c, _):
                work(c * 1024, 1024, False)
                return 0

            with jax.named_scope("chunks"):
                lax.fori_loop(0, inner // 4, whole, 0)

                @pl.when(inner % 4 == 2)
                def _():
                    work(inner // 4 * 1024, 512, False)

                @pl.when(rest >= 2)
                def _():
                    work(inner * 256, 512, True)

                @pl.when(rest % 2 == 1)
                def _():
                    work((chunks - 1) * 256, 256, True)

            dqout[m] = accq[...].T.astype(BF16)

            def back(j, _):
                put(
                    dqout.at[m, rows_of(j), :], dqr.at[par, head],
                    dq_send, dq_recv.at[par], 2 * p + j, spare16.at[4],
                )
                return 0

            lax.fori_loop(0, 2, back, 0)
            lax.fori_loop(*done_after(i), give, 0)

            @pl.when(i > LAG - 1)
            def _():
                finish_all(*done_after(i - LAG))

            return 0

        lax.fori_loop(0, PAIRS, pair_step, 0)
        with jax.named_scope("swap"):
            for i in range(PAIRS - LAG, PAIRS):
                finish_all(*done_after(i))

        with jax.named_scope("worker_waits"):

            wait_for(kv.at[0], fwd_send)
            wait_for(sib_out, sib_send)
            wait_for(kvout, kvs)
            wait_for(dqout, dq_send)

    with jax.named_scope("wait_dq"):
        for i in range(2):
            wait_for(dqr.at[i], dq_recv.at[i])

    part = jnp.zeros((WIN, WIN), F32)
    for h in range(HERE):
        d = (dqr[0, h].astype(F32) + dqr[1, h].astype(F32)) * SCORE_SCALE * gain(qg_ref, h)
        qdn[:, cols(h)] = d
        part = part + qraw[:, cols(h)].astype(F32) * d
    zs[1, 0:1, :] = lanes_to_row(part)
    with jax.named_scope("wait_dk"):
        pltpu.make_async_copy(dkvr.at[0], dkvr.at[0], dkv_recv.at[0]).wait()
    part = jnp.zeros((WIN, WIN), F32)
    for h in range(HERE):
        d = dkvr[0, h].astype(F32) * SCORE_SCALE * gain(kg_ref, h)
        kdn[:, cols(h)] = d
        part = part + kraw[:, cols(h)].astype(F32) * d
    zs[1, 1:2, :] = lanes_to_row(part)
    exchange_z(1)
    with jax.named_scope("wait_dv"):
        pltpu.make_async_copy(dkvr.at[1], dkvr.at[1], dkv_recv.at[1]).wait()
    for h in range(HERE):
        vgrad_ref[:, cols(h)] = dkvr[1, h]
    with jax.named_scope("wait_z2"):
        dots = exchange_z_wait(1) / D
    with jax.named_scope("final"):
        cq = row_to_lanes(dots[0:1, :])
        ck = row_to_lanes(dots[1:2, :])
        for sc, cc, raw, dn, out in (
            (scq, cq, qraw, qdn, qgrad_ref), (sck, ck, kraw, kdn, kgrad_ref),
        ):
            s = sc[...]
            coef = s * s * s * cc
            for h in range(HERE):
                out[:, cols(h)] = (
                    s * dn[:, cols(h)] - raw[:, cols(h)].astype(F32) * coef
                ).astype(BF16)

    with jax.named_scope("ends"):

        for which in range(2):
            wait_for(zx.at[which, pl.ds(0, 7)], z_send.at[which])
        wait_for(st_src, sks)
        lax.fori_loop(PAIRS - WINDOW, PAIRS, turn_sent, 0)
        wait_for(stats.at[pl.ds(0, 6)], ss)


def on_device(q, k, v, fo, do, log_sums, group_index, q_gain, k_gain):
    block = (WIN, HERE * HEAD_DIM)
    any_spec = pl.BlockSpec(memory_space=pl.ANY)
    vmem_spec = pl.BlockSpec(memory_space=pltpu.VMEM)
    dma = pltpu.SemaphoreType.DMA
    return pl.pallas_call(
        kernel,
        out_shape=[pltpu.VMEM(block, BF16)] * 3,
        in_specs=[any_spec] * 9,
        out_specs=[vmem_spec] * 3,
        scratch_shapes=[
            *[pltpu.VMEM(block, BF16)] * 6,
            pltpu.VMEM((WIN, WIN), F32),
            pltpu.VMEM((WIN, WIN), F32),
            pltpu.VMEM((2, KEYS, HEAD_DIM), BF16),
            pltpu.VMEM((8, 2, 2 * WIN, HEAD_DIM), BF16),
            pltpu.VMEM((8, 8, 2 * WIN), F32),
            pltpu.VMEM((HERE, 8, WIN), F32),
            pltpu.VMEM((2, 8, WIN), F32),
            pltpu.VMEM((2, 8, 8, WIN), F32),
            pltpu.VMEM((2, KEYS, HEAD_DIM), F32),
            pltpu.VMEM((HEAD_DIM, 2 * WIN), F32),
            pltpu.VMEM((HEAD_DIM, KEYS), BF16),
            pltpu.VMEM((8, 2 * WIN, HEAD_DIM), BF16),
            pltpu.VMEM((KEYS, HEAD_DIM), BF16),
            pltpu.VMEM((KEYS, HEAD_DIM), BF16),
            pltpu.VMEM((KEYS, HEAD_DIM), BF16),
            pltpu.VMEM((2, HERE, WIN, HEAD_DIM), BF16),
            pltpu.VMEM((2, HERE, WIN, HEAD_DIM), BF16),
            pltpu.VMEM(block, F32),
            pltpu.VMEM(block, F32),
            pltpu.VMEM((512, WIN), F32),
            pltpu.VMEM((BLOCKS, 8, WIN), F32),
            pltpu.VMEM((8, WIN), F32),
            pltpu.VMEM((8, WIN), F32),
            pltpu.VMEM((6, WIN, HEAD_DIM), BF16),
            pltpu.VMEM((2, 8, WIN), F32),
            pltpu.VMEM((HERE, WIN), F32),
            pltpu.VMEM((WINDOWS, WIN), jnp.int32),
            pltpu.VMEM((HERE * HEAD_DIM,), F32),
            pltpu.VMEM((HERE * HEAD_DIM,), F32),
            dma((9,)), dma((2,)), dma((2,)),
            dma, dma, dma((PAIRS, 2)), dma, dma,
            dma, dma((BLOCKS // 2,)), dma, dma((BLOCKS // 2,)),
            dma((8,)), dma, dma, dma((2,)), dma, dma((BLOCKS // 2,)),
            dma, dma((2,)),
        ],
        compiler_params=pltpu.CompilerParams(
            collective_id=0, has_side_effects=True, vmem_limit_bytes=60 << 20
        ),
        cost_estimate=pl.CostEstimate(
            flops=2 * 10**9, bytes_accessed=2 * 10**6, transcendentals=2 * 10**6
        ),
    )(
        q, k, v, fo, do, log_sums, group_index.reshape(WINDOWS, WIN),
        q_gain, k_gain,
    )


def solution(mesh):
    tok, heads = P("tm", "heads"), P("heads")
    return jax.shard_map(
        on_device,
        mesh=mesh,
        in_specs=(tok, tok, tok, tok, tok, P("heads", "tm"), P(), heads, heads),
        out_specs=(tok, tok, tok),
        check_vma=False,
    )
```

time: 72.5 us -> 60.8 us (0.84)
  the two profiles are of different devices: /device:TPU:4 before, /device:TPU:1 now
where the time goes in v2:
time: 60.8 us; the launch traced here: 60.5 us
  Pallas kernels  57.8 us (95%)
  local copies, waits for them, and re-layouts  2.03 us (3%)
  between operations  0.64 us (1%)
    pallas_call x1, Pallas kernels, on_device(): pl.pallas_call(kernel, out_shape=[pltpu.VMEM(block, BF16)] * 3, in_specs=...  57.8 us
    unnamed x3, local copies, waits for them, and re-layouts  2.03 us

profile of v2, /device:TPU:1, one launch (start us, length us, event | category | flops | bytes accessed | tf_op | source)
XLA Modules:
  0.0 60.5 jit_solution(16421505618325228105)
XLA Ops:
  0.6 57.8 %shard_map.112 = (bf16[128,768]{1,0:T(8,128)(2,1)S(1)}, bf16[128,768]{1,0:T(8,128)(2,1)S(1)}, bf16[128,768]{1,0:T(8,128)(2,1)S(1)}) custom-call(bf16[128,768]{1,0:T(8,128)(2,1)} %q_hbm.1, bf16[128,768]{1,0:T(8,128)(2,1)} %k_hbm.1, bf16[128,768]{1,0:T(8,128)(2,1)} %v_hbm.1, bf16[128,768]{1,0:T(8,128)(2,1)} %fo_hbm.1, bf16[128,768]{1,0:T(8,128)(2,1)} %do_hbm.1, ...), custom_call_target="tpu_custom_call" | custom-call | flops 2000000000 | bytes 2000000 | tf_op jit(solution)/shard_map/pallas_call | solution.py:479
  58.4 0.7 %copy.15 = bf16[128,768]{1,0:T(8,128)(2,1)} copy(bf16[128,768]{1,0:T(8,128)(2,1)S(1)} %get-tuple-element.3) | data formatting | bytes 393216
  59.1 0.7 %copy.16 = bf16[128,768]{1,0:T(8,128)(2,1)} copy(bf16[128,768]{1,0:T(8,128)(2,1)S(1)} %get-tuple-element.4) | data formatting | bytes 393216
  59.8 0.7 %copy.17 = bf16[128,768]{1,0:T(8,128)(2,1)} copy(bf16[128,768]{1,0:T(8,128)(2,1)S(1)} %get-tuple-element.5) | data formatting | bytes 393216

commit v3 on v2

--- a/solution.py
+++ b/solution.py
@@ -16,8 +16,8 @@
 WINDOWS = 32
 BLOCKS = WINDOWS // 2
 KEYS = BLOCKS * WIN
-LEAD = 4
-WINDOW = 2
+LEAD = 5
+WINDOW = 4
 LAG = 2
 PAIRS = 8
 MESH = pl.DeviceIdType.MESH
@@ -55,7 +55,7 @@
 
 def kernel(
     q_hbm, k_hbm, v_hbm, fo_hbm, do_hbm, ls_hbm, grp_hbm, qg_hbm, kg_hbm,
-    qgrad_ref, kgrad_ref, vgrad_ref,
+    grads_ref,
     qraw, kraw, vraw, foraw, doraw, qn, scq, sck,
     kv, qd, stats, st_src, zs, zx, acc, accq, kt, dqout, sib_out, sib_in, kvout,
     dqr, dkvr, qdn, kdn,
@@ -266,7 +266,7 @@
     def _():
         with jax.named_scope("wait_kv"):
             acc[...] = jnp.zeros_like(acc)
-            r = lax.broadcasted_iota(jnp.int32, (512, WIN), 0)
+            r = lax.broadcasted_iota(jnp.int32, (1024, WIN), 0)
             place[...] = (r + WIN * (r // WIN)).astype(F32)
 
             @pl.when(core == 0)
@@ -355,44 +355,37 @@
                 wait_for(qd.at[m], qd_recv.at[m])
             accq[...] = jnp.zeros_like(accq)
 
-            def work(row, size, edge):
+            def work(row, size):
                 rows = pl.ds(pl.multiple_of(row, 256), size)
                 q = qd[m, 0]
                 do = qd[m, 1]
                 s = dot(kv[0, rows, :], q, NT)
                 probs = jnp.exp2(s * (SCORE_SCALE * LOG2E) - stats[m, 0:1, :])
-                if edge:
-                    limit = stats[m, 2:3, :] - (2 * row + par * WIN).astype(F32)
-                    at = place[:size, :]
-                    probs = jnp.where(jnp.concatenate([at, at], axis=1) <= limit, probs, 0.0)
+                limit = stats[m, 2:3, :] - (2 * row + par * WIN).astype(F32)
+                at = place[:size, :]
+                probs = jnp.where(jnp.concatenate([at, at], axis=1) <= limit, probs, 0.0)
                 dp = dot(kv[1, rows, :], do, NT)
                 ds = (probs * (dp - stats[m, 1:2, :])).astype(BF16)
                 acc[1, rows, :] += dot(probs.astype(BF16), do, NN)
                 acc[0, rows, :] += dot(ds, q, NN)
                 accq[...] += dot(kt[:, rows], ds, NN)
 
-            chunks = jnp.minimum((p + 3 - par) // 2, BLOCKS // 2)
-            inner = p // 4 * 2
-            rest = chunks - inner
+            blocks = jnp.minimum((p + 3 - par) // 2, BLOCKS // 2)
 
             def whole(c, _):
-                work(c * 1024, 1024, False)
+                work(c * 1024, 1024)
                 return 0
 
             with jax.named_scope("chunks"):
-                lax.fori_loop(0, inner // 4, whole, 0)
-
-                @pl.when(inner % 4 == 2)
+                lax.fori_loop(0, blocks // 4, whole, 0)
+
+                @pl.when(blocks // 2 % 2 == 1)
                 def _():
-                    work(inner // 4 * 1024, 512, False)
-
-                @pl.when(rest >= 2)
+                    work(blocks // 4 * 1024, 512)
+
+                @pl.when(blocks % 2 == 1)
                 def _():
-                    work(inner * 256, 512, True)
-
-                @pl.when(rest % 2 == 1)
-                def _():
-                    work((chunks - 1) * 256, 256, True)
+                    work((blocks - 1) * 256, 256)
 
             dqout[m] = accq[...].T.astype(BF16)
 
@@ -446,19 +439,19 @@
     with jax.named_scope("wait_dv"):
         pltpu.make_async_copy(dkvr.at[1], dkvr.at[1], dkv_recv.at[1]).wait()
     for h in range(HERE):
-        vgrad_ref[:, cols(h)] = dkvr[1, h]
+        grads_ref[2, :, cols(h)] = dkvr[1, h]
     with jax.named_scope("wait_z2"):
         dots = exchange_z_wait(1) / D
     with jax.named_scope("final"):
         cq = row_to_lanes(dots[0:1, :])
         ck = row_to_lanes(dots[1:2, :])
         for sc, cc, raw, dn, out in (
-            (scq, cq, qraw, qdn, qgrad_ref), (sck, ck, kraw, kdn, kgrad_ref),
+            (scq, cq, qraw, qdn, 0), (sck, ck, kraw, kdn, 1),
         ):
             s = sc[...]
             coef = s * s * s * cc
             for h in range(HERE):
-                out[:, cols(h)] = (
+                grads_ref[out, :, cols(h)] = (
                     s * dn[:, cols(h)] - raw[:, cols(h)].astype(F32) * coef
                 ).astype(BF16)
 
@@ -476,11 +469,11 @@
     any_spec = pl.BlockSpec(memory_space=pl.ANY)
     vmem_spec = pl.BlockSpec(memory_space=pltpu.VMEM)
     dma = pltpu.SemaphoreType.DMA
-    return pl.pallas_call(
+    grads = pl.pallas_call(
         kernel,
-        out_shape=[pltpu.VMEM(block, BF16)] * 3,
+        out_shape=pltpu.VMEM((3, *block), BF16),
         in_specs=[any_spec] * 9,
-        out_specs=[vmem_spec] * 3,
+        out_specs=vmem_spec,
         scratch_shapes=[
             *[pltpu.VMEM(block, BF16)] * 6,
             pltpu.VMEM((WIN, WIN), F32),
@@ -502,7 +495,7 @@
             pltpu.VMEM((2, HERE, WIN, HEAD_DIM), BF16),
             pltpu.VMEM(block, F32),
             pltpu.VMEM(block, F32),
-            pltpu.VMEM((512, WIN), F32),
+            pltpu.VMEM((1024, WIN), F32),
             pltpu.VMEM((BLOCKS, 8, WIN), F32),
             pltpu.VMEM((8, WIN), F32),
             pltpu.VMEM((8, WIN), F32),
@@ -528,6 +521,7 @@
         q, k, v, fo, do, log_sums, group_index.reshape(WINDOWS, WIN),
         q_gain, k_gain,
     )
+    return grads[0], grads[1], grads[2]
 
 
 def solution(mesh):

time: 60.8 us -> 56 us (0.921)
  Pallas kernels: 57.8 us -> 54.4 us
  local copies, waits for them, and re-layouts: 2.03 us -> 0.82 us
    pallas_call x1, Pallas kernels: 57.8 us -> 54.4 us  [on_device(): pl.pallas_call(kernel, out_shape=pltpu.VMEM((3, *block), BF16), in_specs=...]
    unnamed x3 -> x0, local copies, waits for them, and re-layouts: 2.03 us -> none
    squeeze x0 -> x1, local copies, waits for them, and re-layouts: none -> 0.82 us  [on_device(): return (grads[0], grads[1], grads[2])]
where the time goes in v3:
time: 56 us; the launch traced here: 55.9 us
  Pallas kernels  54.4 us (97%)
  local copies, waits for them, and re-layouts  0.82 us (1%)
  between operations  0.64 us (1%)
    pallas_call x1, Pallas kernels, on_device(): pl.pallas_call(kernel, out_shape=pltpu.VMEM((3, *block), BF16), in_specs=...  54.4 us

profile of v3, /device:TPU:1, one launch (start us, length us, event | category | flops | bytes accessed | tf_op | source)
XLA Modules:
  0.0 55.9 jit_solution(11870502848002603064)
XLA Ops:
  0.6 54.4 %shard_map.112 = bf16[3,128,768]{2,1,0:T(8,128)(2,1)S(1)} custom-call(bf16[128,768]{1,0:T(8,128)(2,1)} %q_hbm.1, bf16[128,768]{1,0:T(8,128)(2,1)} %k_hbm.1, bf16[128,768]{1,0:T(8,128)(2,1)} %v_hbm.1, bf16[128,768]{1,0:T(8,128)(2,1)} %fo_hbm.1, bf16[128,768]{1,0:T(8,128)(2,1)} %do_hbm.1, f32[6,128]{1,0:T(8,128)} %ls_hbm.1, s32[32,128]{1,0:T(8,128)} %bitcast.7, ...), custom_call_target="tpu_custom_call" | custom-call | flops 2000000000 | bytes 2000000 | tf_op jit(solution)/shard_map/pallas_call | solution.py:472
  55.1 0.8 %slice_bitcast_fusion = (bf16[128,768]{1,0:T(8,128)(2,1)}, bf16[128,768]{1,0:T(8,128)(2,1)}, bf16[128,768]{1,0:T(8,128)(2,1)}) fusion(bf16[3,128,768]{2,1,0:T(8,128)(2,1)S(1)} %shard_map.112), kind=kLoop, calls=%fused_computation | loop fusion | bytes 1179648 | tf_op jit(solution)/shard_map/squeeze | solution.py:524

commit v4 on v3

--- a/solution.py
+++ b/solution.py
@@ -16,8 +16,9 @@
 WINDOWS = 32
 BLOCKS = WINDOWS // 2
 KEYS = BLOCKS * WIN
-LEAD = 5
-WINDOW = 4
+LEAD = 6
+WINDOW = 6
+FIRST = 4
 LAG = 2
 PAIRS = 8
 MESH = pl.DeviceIdType.MESH
@@ -61,7 +62,7 @@
     dqr, dkvr, qdn, kdn,
     place, k_rows, kst_src, gains, spare16, spare32, ls_ref, grp_ref, qg_ref, kg_ref,
     load_sem, z_send, z_recv, sk, sv, sq, ss, sks, kst_recv, kv_recv, fwd_send, fwd_recv,
-    qd_recv, st_recv, dq_send, dq_recv, sib_send, sib_recv, kvs, dkv_recv,
+    qd_recv, st_recv, dq_send, dq_recv, keys_left, sib_send, sib_recv, kvs, dkv_recv,
 ):
     t = lax.axis_index("tm")
     z = lax.axis_index("heads")
@@ -144,11 +145,11 @@
             pltpu.make_async_remote_copy(
                 src_ref=zs.at[which], dst_ref=zx.at[which, z],
                 send_sem=z_send.at[which], recv_sem=z_recv.at[which],
-                device_id={"heads": (z + i) % 8}, device_id_type=MESH,
+                device_id={"heads": (z + 1 + (i + 3) % 7) % 8}, device_id_type=MESH,
             ).start()
             return 0
 
-        lax.fori_loop(1, 8, send, 0)
+        lax.fori_loop(0, 7, send, 0)
         zx[which, pl.ds(z, 1)] = zs[pl.ds(which, 1)]
 
     def exchange_z_wait(which):
@@ -260,7 +261,7 @@
         wait_for(kraw, sk)
         wait_for(vraw, sv)
     with jax.named_scope("send_q0"):
-        lax.fori_loop(0, jnp.where(is_worker, LEAD, PAIRS), send_turn, 0)
+        lax.fori_loop(0, jnp.where(is_worker, FIRST, PAIRS), send_turn, 0)
 
     @pl.when(is_worker)
     def _():
@@ -293,6 +294,7 @@
 
             lax.fori_loop(0, BLOCKS // 2, forward, 0)
 
+        lax.fori_loop(FIRST, LEAD, send_turn, 0)
         with jax.named_scope("forward"):
 
             def forwarded(c, _):
@@ -407,15 +409,20 @@
 
         lax.fori_loop(0, PAIRS, pair_step, 0)
         with jax.named_scope("swap"):
-            for i in range(PAIRS - LAG, PAIRS):
-                finish_all(*done_after(i))
-
-        with jax.named_scope("worker_waits"):
-
-            wait_for(kv.at[0], fwd_send)
-            wait_for(sib_out, sib_send)
-            wait_for(kvout, kvs)
-            wait_for(dqout, dq_send)
+            finish_all(*done_after(PAIRS - 2))
+
+            @pl.when(core == 1)
+            def _():
+                pl.semaphore_wait(keys_left, 1)
+
+            finish_all(*done_after(PAIRS - 1))
+
+            @pl.when(core == 0)
+            def _():
+                wait_for(kvout, kvs)
+                pl.semaphore_signal(
+                    keys_left, inc=1, device_id={"tm": sibling}, device_id_type=MESH
+                )
 
     with jax.named_scope("wait_dq"):
         for i in range(2):
@@ -456,6 +463,14 @@
                 ).astype(BF16)
 
     with jax.named_scope("ends"):
+
+        @pl.when(is_worker)
+        def _():
+            wait_for(kv.at[0], fwd_send)
+            wait_for(sib_out, sib_send)
+            pl.when(core == 1)(functools.partial(wait_for, kvout, kvs))
+            wait_for(dqout, dq_send)
+
 
         for which in range(2):
             wait_for(zx.at[which, pl.ds(0, 7)], z_send.at[which])
@@ -508,7 +523,7 @@
             dma((9,)), dma((2,)), dma((2,)),
             dma, dma, dma((PAIRS, 2)), dma, dma,
             dma, dma((BLOCKS // 2,)), dma, dma((BLOCKS // 2,)),
-            dma((8,)), dma, dma, dma((2,)), dma, dma((BLOCKS // 2,)),
+            dma((8,)), dma, dma, dma((2,)), pltpu.SemaphoreType.REGULAR, dma, dma((BLOCKS // 2,)),
             dma, dma((2,)),
         ],
         compiler_params=pltpu.CompilerParams(

time: 56 us -> 54.9 us (0.980); the launches traced: 55.9 us -> 54.2 us
  Pallas kernels: 54.4 us -> 52.7 us
    pallas_call x1, Pallas kernels: 54.4 us -> 52.7 us  [on_device(): pl.pallas_call(kernel, out_shape=pltpu.VMEM((3, *block), BF16), in_specs=...]
where the time goes in v4:
time: 54.9 us; the launch traced here: 54.2 us
  Pallas kernels  52.7 us (96%)
  local copies, waits for them, and re-layouts  0.82 us (1%)
  between operations  0.64 us (1%)
    pallas_call x1, Pallas kernels, on_device(): pl.pallas_call(kernel, out_shape=pltpu.VMEM((3, *block), BF16), in_specs=...  52.7 us

profile of v4, /device:TPU:1, one launch (start us, length us, event | category | flops | bytes accessed | tf_op | source)
XLA Modules:
  0.0 54.2 jit_solution(13029056568986022256)
XLA Ops:
  0.6 52.7 %shard_map.112 = bf16[3,128,768]{2,1,0:T(8,128)(2,1)S(1)} custom-call(bf16[128,768]{1,0:T(8,128)(2,1)} %q_hbm.1, bf16[128,768]{1,0:T(8,128)(2,1)} %k_hbm.1, bf16[128,768]{1,0:T(8,128)(2,1)} %v_hbm.1, bf16[128,768]{1,0:T(8,128)(2,1)} %fo_hbm.1, bf16[128,768]{1,0:T(8,128)(2,1)} %do_hbm.1, f32[6,128]{1,0:T(8,128)} %ls_hbm.1, s32[32,128]{1,0:T(8,128)} %bitcast.7, ...), custom_call_target="tpu_custom_call" | custom-call | flops 2000000000 | bytes 2000000 | tf_op jit(solution)/shard_map/pallas_call | solution.py:487
  53.4 0.8 %slice_bitcast_fusion = (bf16[128,768]{1,0:T(8,128)(2,1)}, bf16[128,768]{1,0:T(8,128)(2,1)}, bf16[128,768]{1,0:T(8,128)(2,1)}) fusion(bf16[3,128,768]{2,1,0:T(8,128)(2,1)S(1)} %shard_map.112), kind=kLoop, calls=%fused_computation | loop fusion | bytes 1179648 | tf_op jit(solution)/shard_map/squeeze | solution.py:539

commit v5 on v4

--- a/solution.py
+++ b/solution.py
@@ -16,7 +16,7 @@
 WINDOWS = 32
 BLOCKS = WINDOWS // 2
 KEYS = BLOCKS * WIN
-LEAD = 6
+LEAD = 5
 WINDOW = 6
 FIRST = 4
 LAG = 2
@@ -82,21 +82,23 @@
             )
         )
     ]
-    for c in loads:
-        c.start()
     barrier = pltpu.get_barrier_semaphore()
 
     def greet_tm(i, _):
-        pl.semaphore_signal(barrier, inc=1, device_id={"tm": (t + i) % WINDOWS}, device_id_type=MESH)
+        other = (t + 1 + (i + 15) % (WINDOWS - 1)) % WINDOWS
+        pl.semaphore_signal(barrier, inc=1, device_id={"tm": other}, device_id_type=MESH)
         return 0
 
     def greet_z(i, _):
-        pl.semaphore_signal(barrier, inc=1, device_id={"heads": (z + i) % 8}, device_id_type=MESH)
+        other = (z + 1 + (i + 3) % 7) % 8
+        pl.semaphore_signal(barrier, inc=1, device_id={"heads": other}, device_id_type=MESH)
         return 0
 
     with jax.named_scope("greet"):
-        lax.fori_loop(1, 8, greet_z, 0)
-        lax.fori_loop(1, WINDOWS, greet_tm, 0)
+        lax.fori_loop(0, 7, greet_z, 0)
+        lax.fori_loop(0, WINDOWS - 1, greet_tm, 0)
+        for c in loads:
+            c.start()
 
     def cols(h):
         return slice(h * HEAD_DIM, (h + 1) * HEAD_DIM)
@@ -196,14 +198,13 @@
 
         lax.fori_loop(0, 16, step, 0)
 
-    def send_keys(base, h, part):
+    def send_keys(which, src, sem, base, h, part):
         @pl.when(part == own_part)
         def _():
-            for which, src, sem in ((0, kraw, sk), (1, vraw, sv)):
-                put(
-                    src.at[:, head_cols(h)], kv.at[which, rows_of(own_slot), :],
-                    sem, kv_recv.at[own_slot // 2], base + which, spare16.at[which],
-                )
+            put(
+                src.at[:, head_cols(h)], kv.at[which, rows_of(own_slot), :],
+                sem, kv_recv.at[own_slot // 2], base + which, spare16.at[which],
+            )
 
     def send_rows(base, h, part):
         @pl.when(part == own_part)
@@ -223,7 +224,8 @@
             )
 
     with jax.named_scope("send_kv"):
-        for_workers(send_keys)
+        for_workers(functools.partial(send_keys, 0, kraw, sk))
+        for_workers(functools.partial(send_keys, 1, vraw, sv))
 
     with jax.named_scope("wait_z"):
         totals = exchange_z_wait(0)

time: 54.9 us -> 54.8 us (level)
  no operation moved by 1% of the time
where the time goes in v5:
time: 54.8 us; the launch traced here: 54.2 us
  Pallas kernels  52.7 us (96%)
  local copies, waits for them, and re-layouts  0.82 us (1%)
  between operations  0.64 us (1%)
    pallas_call x1, Pallas kernels, on_device(): pl.pallas_call(kernel, out_shape=pltpu.VMEM((3, *block), BF16), in_specs=...  52.7 us

profile of v5, /device:TPU:1, one launch (start us, length us, event | category | flops | bytes accessed | tf_op | source)
XLA Modules:
  0.0 54.2 jit_solution(2088290019018308624)
XLA Ops:
  0.6 52.7 %shard_map.112 = bf16[3,128,768]{2,1,0:T(8,128)(2,1)S(1)} custom-call(bf16[128,768]{1,0:T(8,128)(2,1)} %q_hbm.1, bf16[128,768]{1,0:T(8,128)(2,1)} %k_hbm.1, bf16[128,768]{1,0:T(8,128)(2,1)} %v_hbm.1, bf16[128,768]{1,0:T(8,128)(2,1)} %fo_hbm.1, bf16[128,768]{1,0:T(8,128)(2,1)} %do_hbm.1, f32[6,128]{1,0:T(8,128)} %ls_hbm.1, s32[32,128]{1,0:T(8,128)} %bitcast.7, ...), custom_call_target="tpu_custom_call" | custom-call | flops 2000000000 | bytes 2000000 | tf_op jit(solution)/shard_map/pallas_call | solution.py:489
  53.3 0.8 %slice_bitcast_fusion = (bf16[128,768]{1,0:T(8,128)(2,1)}, bf16[128,768]{1,0:T(8,128)(2,1)}, bf16[128,768]{1,0:T(8,128)(2,1)}) fusion(bf16[3,128,768]{2,1,0:T(8,128)(2,1)S(1)} %shard_map.112), kind=kLoop, calls=%fused_computation | loop fusion | bytes 1179648 | tf_op jit(solution)/shard_map/squeeze | solution.py:541
